TPU v7x, 32 devices: a whole 2x2x4 slice. The times are simulated.
32 devices in a mesh: group: 4 (over x, core), inner: 8 (over z, y).
Axes of the slice: x: 2, y: 2, z: 4, core: 2. Of those that a mesh axis runs over, the one named last changes fastest.
Arguments:
- flow_field: float32 [1536, 1536, 128], P('inner', 'group'), may hold values from -6 to 6
- sketch_rows: float32 [1536, 128], P('inner'), may hold values from -6 to 6
- sketch_cols: float32 [1536, 128], P('group'), may hold values from -6 to 6
- sketch_depth: float32 [128, 128], replicated, may hold values from -6 to 6
- bit_widths: int32 [2], replicated, may hold values from 6 to 8
- bin_edges: int32 [9], replicated, may hold values from -6 to 6, as said below
Outputs:
- basis_one: float32 [1536, 128], P('inner')
- basis_two: float32 [1536, 128], P('group')
- core: float32 [128, 128, 128], P('inner', 'group')
- residual: float32 [2, 128, 128, 128], P(None, 'inner', 'group')
- energy: float32 [2, 1536, 128], P(None, 'inner')
- histogram: float32 [2, 1536, 8], P(None, 'inner')
Inputs may be any that keep to these rules, and one draw needn't show every extreme that they name: `bin_edges`: strictly increasing; the first is -6 and the last 6.
All inputs are finite; a program needn't handle non-finite values.
Results may differ from a plain program's by a relative error of at most 0.0008.
Values sent between devices are 32-bit elements; how exact they have to be, the bound alone decides.
A program may use at most 128 MiB of HBM per device.

v0:
```python
import math

import jax
import jax.numpy as jnp
from jax import lax
from jax.sharding import PartitionSpec as P

N1 = 1536
N2 = 1536
N3 = 128
R = 128
NEDGE = 9
NBINS = 8


precise = lax.Precision.HIGHEST
two_pi = 2.0 * 3.141592653589793
error_boost = 16.0


def gram_of(sketch):
    return jnp.dot(sketch.T, sketch, precision=precise)


def orthonormal_rows(sketch, gram_matrix):
    lower_factor = jnp.linalg.cholesky(gram_matrix)
    return jax.scipy.linalg.solve_triangular(lower_factor, sketch.T, lower=True).T


def soft_residual(core_values, step_size):
    return -jnp.sin(two_pi * core_values[None] / step_size[:, None, None, None]) / two_pi


def local(flow_field, sketch_rows, sketch_cols, sketch_depth, bit_widths, bin_edges):
    reduced = jnp.einsum("ijk,kr->ijr", flow_field, sketch_depth, precision=precise)
    mode_one = jnp.einsum("ijr,jr->ir", reduced, sketch_cols, precision=precise)
    mode_two = jnp.einsum("ijr,ir->jr", reduced, sketch_rows, precision=precise)
    mode_one = lax.psum(mode_one, "group")
    basis_one = orthonormal_rows(mode_one, lax.psum(gram_of(mode_one), "inner"))
    mode_two = lax.psum(mode_two, "inner")
    basis_two = orthonormal_rows(mode_two, lax.psum(gram_of(mode_two), "group"))
    along_two = jnp.einsum("ijk,js->isk", flow_field, basis_two, precision=precise)
    levels = jnp.exp2(bit_widths.astype(jnp.float32) - 1.0) - 1.0
    summed_two = lax.psum_scatter(along_two, "group", scatter_dimension=1, tiled=True)
    partial_rows = jnp.einsum("ir,isk->rsk", basis_one, summed_two, precision=precise)
    core_shard = lax.psum_scatter(partial_rows, "inner", scatter_dimension=0, tiled=True)
    peak = lax.pmax(jnp.max(jnp.abs(core_shard)), ("group", "inner"))
    residual_shard = soft_residual(core_shard, peak / levels)
    spread = lax.all_gather(residual_shard, "group", axis=2, tiled=True)
    mixed_core = jnp.einsum(
        "ir,brsk->bisk",
        basis_one,
        lax.all_gather(spread, "inner", axis=1, tiled=True),
        precision=precise,
    )
    error_scale = error_boost * math.sqrt(N1 * N2) / R
    field_error = error_scale * jnp.einsum(
        "bisk,js->bijk", mixed_core, basis_two, precision=precise
    )
    energy_part = jnp.sum(field_error * field_error, axis=2) / N2
    edge_values = bin_edges.astype(jnp.float32)
    ramp_part = jnp.stack(
        [
            jnp.sum(jnp.clip(field_error - edge_values[index_edge] + 0.5, 0.0, 1.0), axis=(2, 3))
            for index_edge in range(NEDGE)
        ],
        axis=-1,
    )
    energy, ramp_sums = lax.psum((energy_part, ramp_part), "group")
    histogram = (ramp_sums[..., :-1] - ramp_sums[..., 1:]) * (NBINS / (N2 * N3))
    return (basis_one, basis_two, core_shard, residual_shard, energy, histogram)


def solution(mesh):
    in_specs = (P("inner", "group", None), P("inner", None), P("group", None), P(), P(), P())
    out_specs = (
        P("inner", None),
        P("group", None),
        P("inner", "group", None),
        P(None, "inner", "group", None),
        P(None, "inner", None),
        P(None, "inner", None),
    )
    return jax.shard_map(local, mesh=mesh, in_specs=in_specs, out_specs=out_specs, check_vma=False)
```

profile of v0, /device:TPU:0, one launch (start us, length us, event | category | flops | bytes accessed | tf_op | source)
XLA Modules:
  0.0 1027.6 jit_solution(7417091754691610405)
XLA Ops:
  8.0 36.0 %multiply_reduce_fusion.2 = (f32[128,192]{0,1:T(8,128)S(1)}, f32[192,384,128]{2,1,0:T(8,128)}) fusion(f32[128,384]{0,1:T(8,128)} %bitcast.94, f32[192,384,128]{2,1,0:T(8,128)} %param.7, f32[128,128]{1,0:T(8,128)S(1)} %copy-done), kind=kOutput, calls=%fused_computation.11 | convolution fusion | flops 14514364416 | bytes 75857920 | tf_op jit(solution)/shard_map/ijk,kr->ijr/dot_general | solution.py:35
  44.9 14.0 %multiply_reduce_fusion.1 = f32[128,384]{0,1:T(8,128)S(1)} fusion(f32[192,384,128]{2,1,0:T(8,128)} %get-tuple-element.43, f32[128,192]{0,1:T(8,128)S(1)} %bitcast.99), kind=kLoop, calls=%fused_computation.10 | loop fusion | flops 18825216 | bytes 38043648
  59.7 19.4 %all-reduce.6.cloned.1.call-done = f32[192,128]{0,1:T(8,128)} async-done(((f32[192,128]{0,1:T(8,128)}), f32[192,128]{0,1:T(8,128)}) %all-reduce.6.cloned.1.call-update) | async-done | bytes 98320 | tf_op jit(solution)/shard_map/psum | solution.py:38
  79.1 1.9 fusion.25
  81.0 73.3 %all-reduce.12.cloned.1.call-done = (f32[128,128]{0,1:T(8,128)}, f32[384,128]{0,1:T(8,128)}) async-done(((f32[128,128]{0,1:T(8,128)}, f32[384,128]{0,1:T(8,128)}), (f32[128,128]{0,1:T(8,128)}, f32[384,128]{0,1:T(8,128)})) %all-reduce.12.cloned.1.call-update) | async-done | bytes 262160 | tf_op jit(solution)/shard_map/psum | solution.py:39
  154.3 2.0 fusion.26
  156.8 30.9 %all-reduce.8.cloned.1.call-done = f32[128,128]{0,1:T(8,128)} async-done(((f32[128,128]{0,1:T(8,128)}), f32[128,128]{0,1:T(8,128)}) %all-reduce.8.cloned.1.call-update) | async-done | bytes 65552 | tf_op jit(solution)/shard_map/psum | solution.py:41
  189.4 11.7 %cholesky.55 = f32[128,128]{1,0:T(8,128)S(1)} custom-call(f32[128,128]{1,0:T(8,128)S(1)} %fusion.17), custom_call_target="Cholesky" | custom-call | tf_op jit(solution)/shard_map/jit(cholesky)/cholesky | solution.py:26
  202.5 9.8 custom-call.11
  213.6 32.7 %fusion.8 = f32[128,192,128]{2,0,1:T(8,128)} fusion(f32[192,384,128]{2,1,0:T(8,128)} %param.7, f32[128,384]{1,0:T(8,128)S(1)} %fusion.15), kind=kOutput, calls=%fused_computation.24 | convolution fusion | flops 14495514624 | bytes 50528256 | tf_op jit(solution)/shard_map/ijk,js->isk/dot_general | solution.py:42
  246.3 16.5 %copy.62 = f32[128,192,128]{2,1,0:T(8,128)} copy(f32[128,192,128]{2,0,1:T(8,128)} %fusion.8) | data formatting | bytes 25165824 | tf_op jit(solution)/shard_map/ijk,js->isk/dot_general | solution.py:42
  263.3 11.7 %cholesky.44 = f32[128,128]{1,0:T(8,128)S(1)} custom-call(f32[128,128]{1,0:T(8,128)S(1)} %fusion.20), custom_call_target="Cholesky" | custom-call | tf_op jit(solution)/shard_map/jit(cholesky)/cholesky | solution.py:26
  276.3 9.8 custom-call.10
  286.5 75.6 %reduce-scatter.3.cloned.1.call-done = f32[192,32,128]{2,0,1:T(8,128)} async-done(((f32[192,128,128]{2,0,1:T(8,128)}), f32[192,32,128]{2,0,1:T(8,128)}) %reduce-scatter.3.cloned.1.call-update) | async-done | bytes 3145744 | tf_op jit(solution)/shard_map/reduce_scatter | solution.py:44
  362.1 5.2 fusion.11
  367.4 68.2 %reduce-scatter.5.cloned.1.call-done = f32[16,32,128]{2,0,1:T(8,128)} async-done(((f32[128,32,128]{2,0,1:T(8,128)}), f32[16,32,128]{2,0,1:T(8,128)}) %reduce-scatter.5.cloned.1.call-update) | async-done | bytes 262160 | tf_op jit(solution)/shard_map/reduce_scatter | solution.py:46
  437.3 39.8 %pmax.7 = f32[]{:T(128)} all-reduce(f32[]{:T(128)} %get-tuple-element.32), channel_id=1, replica_groups=mesh['group'=4,'inner'=8] {'group','inner'}, use_global_device_ids=true, to_apply=%region_9.11 | all-reduce | flops 1 | bytes 8 | tf_op jit(solution)/shard_map/pmax | solution.py:47
  477.8 2.6 fusion.6
  480.4 22.3 %all-gather.3.cloned.1.call-done = f32[2,16,128,128]{3,2,1,0:T(8,128)} async-done(((f32[2,16,32,128]{3,2,1,0:T(8,128)}), f32[2,16,128,128]{3,2,1,0:T(8,128)}) %all-gather.3.cloned.1.call-update) | async-done | bytes 2097168 | tf_op jit(solution)/shard_map/all_gather | solution.py:49
  506.3 226.5 %all-gather.5.cloned.1.call-done = f32[2,128,128,128]{3,2,1,0:T(8,128)} async-done(((f32[2,16,128,128]{3,2,1,0:T(8,128)}), f32[2,128,128,128]{3,2,1,0:T(8,128)}) %all-gather.5.cloned.1.call-update) | async-done | bytes 16777232 | tf_op jit(solution)/shard_map/all_gather | solution.py:53
  732.8 35.8 %fusion.3 = f32[2,128,128,192]{2,3,1,0:T(8,128)S(1)} fusion(f32[2,128,128,128]{3,2,1,0:T(8,128)} %all-gather.5.cloned.1.call-done, f32[128,192]{0,1:T(8,128)S(1)} %fusion.18), kind=kOutput, calls=%fused_computation.16 | convolution fusion | flops 9663676416 | bytes 42041344 | tf_op jit(solution)/shard_map/ir,brsk->bisk/dot_general | solution.py:50
  768.6 209.0 %clamp_reduce_fusion = (f32[2,192]{1,0:T(2,128)S(1)}, f32[2,192]{1,0:T(2,128)S(1)}, f32[2,192]{1,0:T(2,128)S(1)}, f32[2,192]{1,0:T(2,128)S(1)}, f32[2,192]{1,0:T...) fusion(f32[]{:T(128)} %bitcast.38, f32[]{:T(128)} %bitcast.22, ...), kind=kOutput, calls=%fused_computation | convolution fusion | flops 29727076352 | bytes 25572900 | tf_op jit(solution)/shard_map/bisk,js->bijk/dot_general | solution.py:57
  977.7 10.6 %psum.47 = f32[2,192,9]{1,0,2:T(2,128)S(1)} all-reduce(f32[2,192,9]{1,0,2:T(2,128)S(1)} %constant_dynamic-update-slice_fusion), channel_id=1, replica_groups=mesh['group'=4,'inner'=8] {'group'}, use_global_device_ids=true, to_apply=%region_21.23 | all-reduce | flops 3456 | bytes 27648 | tf_op jit(solution)/shard_map/psum | solution.py:69
  989.6 29.2 %all-reduce.10.cloned.1.call-done = f32[2,192,128]{2,1,0:T(8,128)} async-done(((f32[2,192,128]{2,1,0:T(8,128)}), f32[2,192,128]{2,1,0:T(8,128)}) %all-reduce.10.cloned.1.call-update) | async-done | bytes 196624 | tf_op jit(solution)/shard_map/psum | solution.py:69
  (66 shorter events, 18.4 us)
Async XLA Ops:
  7.2 0.8 copy-start
  7.2 71.9 %all-reduce.6.cloned.1.call-start = ((), (), s32[]{:S(2)}) async-start(), calls=%async_computation.2 | async-start | bytes 262144 | tf_op jit(solution)/shard_map/psum | solution.py:38
  8.0 36.9 %copy-start.5 = (f32[192,128]{1,0:T(8,128)S(1)}, f32[192,128]{1,0:T(8,128)}, u32[]{:S(2)}) copy-start(f32[192,128]{1,0:T(8,128)} %param.8) | copy-start | bytes 294916
  44.8 109.5 %all-reduce.12.cloned.1.call-start = ((), (), s32[]{:S(2)}) async-start(), calls=%async_computation.9 | async-start | bytes 524288 | tf_op jit(solution)/shard_map/psum | solution.py:39
  81.0 106.7 %all-reduce.8.cloned.1.call-start = ((), (), s32[]{:S(2)}) async-start(), calls=%async_computation.3 | async-start | bytes 131072 | tf_op jit(solution)/shard_map/psum | solution.py:41
  156.4 205.7 %reduce-scatter.3.cloned.1.call-start = ((), (), s32[]{:S(2)}) async-start(), calls=%async_computation.4 | async-start | bytes 15728640 | tf_op jit(solution)/shard_map/reduce_scatter | solution.py:44
  246.3 16.8 %copy-start.4 = (f32[128,128]{0,1:T(8,128)S(1)}, f32[128,128]{0,1:T(8,128)}, u32[]{:S(2)}) copy-start(f32[128,128]{0,1:T(8,128)} %get-tuple-element.29) | copy-start | bytes 196612
  246.3 39.8 %copy-start.2 = (f32[192,128]{0,1:T(8,128)S(1)}, f32[192,128]{0,1:T(8,128)}, u32[]{:S(2)}) copy-start(f32[192,128]{0,1:T(8,128)} %all-reduce.6.cloned.1.call-done) | copy-start | bytes 294916
  246.3 230.8 %copy-start.6 = (s32[2]{0:T(128)S(1)}, s32[2]{0:T(128)}, u32[]{:S(2)}) copy-start(s32[2]{0:T(128)} %param.11) | copy-start | bytes 28
  246.3 256.8 %copy-start.7 = (s32[9]{0:T(128)S(1)}, s32[9]{0:T(128)}, u32[]{:S(2)}) copy-start(s32[9]{0:T(128)} %param.12) | copy-start | bytes 112
  262.9 172.8 %reduce-scatter.5.cloned.1.call-start = ((), (), s32[]{:S(2)}) async-start(), calls=%async_computation.5 | async-start | bytes 2359296 | tf_op jit(solution)/shard_map/reduce_scatter | solution.py:46
  286.5 691.0 %copy-start.3 = (f32[128,192]{0,1:T(8,128)}, f32[128,192]{0,1:T(8,128)S(1)}, u32[]{:S(2)}) copy-start(f32[128,192]{0,1:T(8,128)S(1)} %fusion.18) | copy-start | bytes 294916
  367.4 135.4 %all-gather.3.cloned.1.call-start = ((), (), s32[]{:S(2)}) async-start(), calls=%async_computation.6 | async-start | bytes 2621440 | tf_op jit(solution)/shard_map/all_gather | solution.py:49
  480.4 252.4 %all-gather.5.cloned.1.call-start = ((), (), s32[]{:S(2)}) async-start(), calls=%async_computation.7 | async-start | bytes 18874368 | tf_op jit(solution)/shard_map/all_gather | solution.py:53
  502.8 516.0 %all-reduce.10.cloned.1.call-start = ((), (), s32[]{:S(2)}) async-start(), calls=%async_computation.8 | async-start | bytes 393216 | tf_op jit(solution)/shard_map/psum | solution.py:69
  768.6 251.8 %copy-start.1 = (f32[128,128]{1,0:T(8,128)S(1)}, f32[128,128]{1,0:T(8,128)}, u32[]{:S(2)}) copy-start(f32[128,128]{1,0:T(8,128)} %param.10) | copy-start | bytes 196612
Sparse Core Ops, SparseCore 0:
  44.9 34.0 all-reduce.5
  83.5 70.7 all-reduce.11
  157.2 30.3 all-reduce.7
  263.0 99.0 reduce-scatter.2
  367.5 68.0 reduce-scatter.4
  480.5 22.2 all-gather.2
  505.2 227.5 all-gather.4
  989.1 29.6 all-reduce.9
where the time goes:
time: 1030 us
  waiting for transfers between devices  545 us (53%)
  matrix products  324 us (31%)
  other arithmetic  66.1 us (6%)
  blocking collectives  50.4 us (5%)
  local copies, waits for them, and re-layouts  25.5 us (2%)
  between operations  14.8 us (1%)
    all_gather x1, waiting for transfers between devices, local(): lax.all_gather(spread, 'inner', axis=1, tiled=True)  226 us
    dot_general x1, matrix products, local(): jnp.einsum('bisk,js->bijk', mixed_core, basis_two, precision=precise)  209 us
    reduce_scatter x1, waiting for transfers between devices, local(): lax.psum_scatter(along_two, 'group', scatter_dimension=1, tiled=True)  75.6 us
    psum x1, waiting for transfers between devices, local(): basis_one = orthonormal_rows(mode_one, lax.psum(gram_of(mode_one), 'inner'))  73.3 us
    reduce_scatter x1, waiting for transfers between devices, local(): lax.psum_scatter(partial_rows, 'inner', scatter_dimension=0, tiled=True)  68.2 us
    pmax x1, blocking collectives, local(): peak = lax.pmax(jnp.max(jnp.abs(core_shard)), ('group', 'inner'))  39.8 us
    dot_general x1, matrix products, local(): jnp.einsum('ijk,kr->ijr', flow_field, sketch_depth, precision=precise)  36 us
    dot_general x1, matrix products, local(): jnp.einsum('ir,brsk->bisk', basis_one, lax.all_gather(spread, 'inner', ax...  35.8 us
  transfers between devices with their start and end apart: 8, of which 8 were waited for; matrix products, arithmetic and copies ran while one was open for 4% of the time, Pallas kernels for 0%

commit v1 on v0

v1 whole, which is shorter than its diff:
```python
import functools
import math

import jax
import jax.numpy as jnp
from jax import lax
from jax.experimental import pallas as pl
from jax.experimental.pallas import tpu as pltpu
from jax.sharding import PartitionSpec as P

NEDGE = 9
NBINS = 8

precise = lax.Precision.HIGHEST
error_boost = 16.0
two_pi = 2.0 * math.pi
sine_terms = [
    (-1.0) ** n * two_pi ** (2 * n) / math.factorial(2 * n + 1) for n in range(7)
]


def soft_residual(core_values, inverse_step):
    turns = core_values * inverse_step
    turns = turns - jnp.round(turns)
    size = jnp.abs(turns)
    folded = jnp.where(size > 0.25, 0.5 - size, size)
    folded = jnp.where(turns < 0.0, folded, -folded)
    square = folded * folded
    value = jnp.full_like(square, sine_terms[-1])
    for term in sine_terms[-2::-1]:
        value = value * square + term
    return folded * value


def error_kernel(low_ref, basis_ref, mixed_ref, out_ref, *, chunk):
    rows = mixed_ref.shape[1]
    depth = mixed_ref.shape[3]
    cells = basis_ref.shape[0]

    def one_row(i, carry):
        wide = jnp.concatenate([mixed_ref[0, i], mixed_ref[1, i]], axis=1)
        high = wide.astype(jnp.bfloat16)
        rest = (wide - high.astype(jnp.float32)).astype(jnp.bfloat16)
        both = jnp.concatenate([high, rest], axis=0)
        sums = [[None] * (NEDGE + 1) for _ in range(2)]
        for start in range(0, cells, chunk):
            error = jnp.dot(
                basis_ref[start : start + chunk, :], both, preferred_element_type=jnp.float32
            )
            for b in range(2):
                part = error[:, b * depth : (b + 1) * depth].reshape(chunk // 8, 8, depth)
                pieces = [
                    jnp.sum(
                        jnp.minimum(jnp.maximum(part, low_ref[e]), low_ref[e] + 1.0), axis=0
                    )
                    for e in range(NEDGE)
                ]
                pieces.append(jnp.sum(part * part, axis=0))
                sums[b] = [p if s is None else s + p for s, p in zip(sums[b], pieces)]
        for b in range(2):
            for e in range(NEDGE):
                shifted = sums[b][e] - (cells // 8) * low_ref[e]
                out_ref[b, i, e : e + 1, :] = jnp.sum(shifted, axis=0, keepdims=True)
            out_ref[b, i, NEDGE : NEDGE + 1, :] = jnp.sum(sums[b][NEDGE], axis=0, keepdims=True)
        return carry

    lax.fori_loop(0, rows, one_row, 0)


def error_sums(low_edges, basis, mixed):
    rows, ranks, depth = mixed.shape[1:]
    cells = basis.shape[0]
    block = math.gcd(rows, 16)
    chunk = math.gcd(cells, 128)
    return pl.pallas_call(
        functools.partial(error_kernel, chunk=chunk),
        grid=(rows // block,),
        in_specs=[
            pl.BlockSpec(memory_space=pltpu.SMEM),
            pl.BlockSpec((cells, 2 * ranks), lambda i: (0, 0)),
            pl.BlockSpec((2, block, ranks, depth), lambda i: (0, i, 0, 0)),
        ],
        out_specs=pl.BlockSpec((2, block, NEDGE + 1, depth), lambda i: (0, i, 0, 0)),
        out_shape=jax.ShapeDtypeStruct((2, rows, NEDGE + 1, depth), jnp.float32),
        compiler_params=pltpu.CompilerParams(vmem_limit_bytes=32 * 1024 * 1024),
    )(low_edges, jnp.concatenate([basis, basis], axis=1), mixed)


def gram_of(sketch):
    return jnp.dot(sketch.T, sketch, precision=precise)


def local(groups, inners, flow_field, sketch_rows, sketch_cols, sketch_depth, bit_widths, bin_edges):
    ranks = sketch_depth.shape[1]
    depth = flow_field.shape[2]
    n1 = flow_field.shape[0] * inners
    n2 = flow_field.shape[1] * groups
    reduced = jnp.einsum("ijk,kr->ijr", flow_field, sketch_depth, precision=precise)
    mode_one = jnp.einsum("ijr,jr->ir", reduced, sketch_cols, precision=precise)
    mode_two = jnp.einsum("ijr,ir->jr", reduced, sketch_rows, precision=precise)
    mode_one = lax.psum(mode_one, "group")
    mode_two = lax.psum(mode_two, "inner")
    gram_one = lax.psum(gram_of(mode_one), "inner")
    gram_two = lax.psum(gram_of(mode_two), "group")
    lower = jnp.linalg.cholesky(jnp.stack([gram_one, gram_two]))
    unit = jnp.broadcast_to(jnp.eye(ranks, dtype=jnp.float32), lower.shape)
    inverse = jax.scipy.linalg.solve_triangular(lower, unit, lower=True)
    basis_one = jnp.einsum("ir,sr->is", mode_one, inverse[0], precision=precise)
    basis_two = jnp.einsum("jr,sr->js", mode_two, inverse[1], precision=precise)
    along_two = jnp.einsum("ijk,js->isk", flow_field, basis_two, precision=precise)
    partial_core = jnp.einsum("ir,isk->rsk", basis_one, along_two, precision=precise)
    partial_core = lax.psum_scatter(partial_core, "group", scatter_dimension=1, tiled=True)
    core_shard = lax.psum_scatter(partial_core, "inner", scatter_dimension=0, tiled=True)
    spread = lax.all_gather(core_shard, "inner", axis=0, tiled=True)
    core = lax.all_gather(spread, "group", axis=1, tiled=True)
    peak = jnp.max(jnp.abs(core))
    levels = jnp.exp2(bit_widths.astype(jnp.float32) - 1.0) - 1.0
    inverse_step = levels / peak
    residual_shard = soft_residual(core_shard[None], inverse_step[:, None, None, None])
    residual = soft_residual(core[None], inverse_step[:, None, None, None])
    mixed = jnp.einsum("ir,brsk->bisk", basis_one, residual, precision=lax.Precision.HIGH)
    error_scale = error_boost * math.sqrt(n1 * n2) / ranks
    sums = error_sums(
        bin_edges.astype(jnp.float32) - 0.5, (error_scale * basis_two).astype(jnp.bfloat16), mixed
    )
    parts = jnp.concatenate(
        [sums[:, :, NEDGE], jnp.sum(sums[:, :, :NEDGE], axis=-1)], axis=-1
    )
    total = lax.psum(parts, "group")
    energy = total[..., :depth] / n2
    ramps = total[..., depth:]
    histogram = (ramps[..., :-1] - ramps[..., 1:]) * (NBINS / (n2 * depth))
    return (basis_one, basis_two, core_shard, residual_shard, energy, histogram)


def solution(mesh):
    in_specs = (P("inner", "group", None), P("inner", None), P("group", None), P(), P(), P())
    out_specs = (
        P("inner", None),
        P("group", None),
        P("inner", "group", None),
        P(None, "inner", "group", None),
        P(None, "inner", None),
        P(None, "inner", None),
    )
    body = functools.partial(local, mesh.shape["group"], mesh.shape["inner"])
    return jax.shard_map(body, mesh=mesh, in_specs=in_specs, out_specs=out_specs, check_vma=False)
```

time: 1030 us -> 762 us (0.74)
  matrix products: 324 us -> 122 us
  waiting for transfers between devices: 545 us -> 406 us
  Pallas kernels: 0 us -> 110 us
  blocking collectives: 50.4 us -> 0 us
    dot_general x3 -> x4, matrix products: 250 us -> 49.3 us  [the longest x1 25.8 us: local(): jnp.einsum('ir,brsk->bisk', basis_one, residual, precision=lax.Precision....]
    all_gather x2, waiting for transfers between devices: 249 us -> 109 us  [the longest x1 56.7 us: local(): core = lax.all_gather(spread, 'group', axis=1, tiled=True)]
    pallas_call x0 -> x1, Pallas kernels: none -> 110 us  [error_sums(): pl.pallas_call(functools.partial(error_kernel, chunk=chunk), grid=(rows /...]
    pmax x1 -> x0, blocking collectives: 39.8 us -> none  [local(): peak = lax.pmax(jnp.max(jnp.abs(core_shard)), ('group', 'inner'))]
    dot_general x1, local copies, waits for them, and re-layouts: 16.5 us -> 29.1 us  [local(): jnp.einsum('ir,brsk->bisk', basis_one, residual, precision=lax.Precision....]
    psum x1 -> x0, blocking collectives: 10.6 us -> none  [local(): energy, ramp_sums = lax.psum((energy_part, ramp_part), 'group')]
    another operation x10 -> x7, other arithmetic: 45.7 us -> 43.4 us  [the longest x4 23.6 us: local(): lower = jnp.linalg.cholesky(jnp.stack([gram_one, gram_two]))]
  transfers between devices with their start and end apart: 8 -> 8, of which waited for: 8 -> 8; matrix products, arithmetic and copies ran while one was open for 4% -> 2% of each run, Pallas kernels for 0% -> 0%
where the time goes in v1:
time: 762 us; the launch traced here: 757 us
  waiting for transfers between devices  406 us (53%)
  matrix products  122 us (16%)
  Pallas kernels  110 us (14%)
  other arithmetic  68.5 us (9%)
  local copies, waits for them, and re-layouts  35.3 us (5%)
  between operations  14.7 us (2%)
    pallas_call x1, Pallas kernels, error_sums(): pl.pallas_call(functools.partial(error_kernel, chunk=chunk), grid=(rows /...  110 us
    psum x1, waiting for transfers between devices, local(): gram_one = lax.psum(gram_of(mode_one), 'inner')  73.2 us
    reduce_scatter x1, waiting for transfers between devices, local(): lax.psum_scatter(partial_core, 'group', scatter_dimension=1, tiled=True)  71.8 us
    reduce_scatter x1, waiting for transfers between devices, local(): lax.psum_scatter(partial_core, 'inner', scatter_dimension=0, tiled=True)  71.8 us
    all_gather x1, waiting for transfers between devices, local(): core = lax.all_gather(spread, 'group', axis=1, tiled=True)  56.7 us
    all_gather x1, waiting for transfers between devices, local(): spread = lax.all_gather(core_shard, 'inner', axis=0, tiled=True)  51.9 us
    dot_general x1, matrix products, local(): jnp.einsum('ijk,kr->ijr', flow_field, sketch_depth, precision=precise)  36.1 us
    dot_general x1, matrix products, local(): jnp.einsum('ijk,js->isk', flow_field, basis_two, precision=precise)  32.2 us
  transfers between devices with their start and end apart: 8, of which 8 were waited for; matrix products, arithmetic and copies ran while one was open for 2% of the time, Pallas kernels for 0%

profile of v1, /device:TPU:0, one launch (start us, length us, event | category | flops | bytes accessed | tf_op | source)
XLA Modules:
  0.0 757.1 jit_solution(15632016935528410060)
XLA Ops:
  8.0 36.1 %multiply_reduce_fusion.1 = (f32[128,192]{0,1:T(8,128)S(1)}, f32[192,384,128]{2,1,0:T(8,128)}) fusion(f32[128,384]{0,1:T(8,128)} %bitcast.58, f32[192,384,128]{2,1,0:T(8,128)} %param.6, f32[128,128]{1,0:T(8,128)S(1)} %copy-done), kind=kOutput, calls=%fused_computation.2 | convolution fusion | flops 14514364416 | bytes 75857920 | tf_op jit(solution)/shard_map/ijk,kr->ijr/dot_general | solution.py:98
  44.9 14.0 %multiply_reduce_fusion = f32[128,384]{0,1:T(8,128)S(1)} fusion(f32[192,384,128]{2,1,0:T(8,128)} %get-tuple-element.27, f32[128,192]{0,1:T(8,128)S(1)} %bitcast.62), kind=kLoop, calls=%fused_computation.1 | loop fusion | flops 18825216 | bytes 38043648
  59.7 19.4 %all-reduce.6.cloned.1.call-done = f32[192,128]{0,1:T(8,128)} async-done(((f32[192,128]{0,1:T(8,128)}), f32[192,128]{0,1:T(8,128)}) %all-reduce.6.cloned.1.call-update) | async-done | bytes 98320 | tf_op jit(solution)/shard_map/psum | solution.py:101
  79.1 1.9 convolution_bitcast_fusion.1
  81.2 73.2 %all-reduce.12.cloned.1.call-done = (f32[1,128,128]{1,2,0:T(8,128)}, f32[384,128]{0,1:T(8,128)}) async-done(((f32[1,128,128]{1,2,0:T(8,128)}, f32[384,128]{0,1:T(8,128)}), (f32[1,128,128]{1,2,0:T(8,128)}, f32[384,128]{0,1:T(8,128)})) %all-reduce.12.cloned.1.call-update) | async-done | bytes 262160 | tf_op jit(solution)/shard_map/psum | solution.py:103
  154.3 2.0 convolution_bitcast_fusion.2
  157.8 29.8 %all-reduce.8.cloned.1.call-done = f32[1,128,128]{1,2,0:T(8,128)} async-done(((f32[1,128,128]{1,2,0:T(8,128)}), f32[1,128,128]{1,2,0:T(8,128)}) %all-reduce.8.cloned.1.call-update) | async-done | bytes 65552 | tf_op jit(solution)/shard_map/psum | solution.py:104
  188.6 23.5 %custom-call.8 = f32[2,128,128]{2,1,0:T(8,128)S(1)} custom-call(f32[2,128,128]{2,1,0:T(8,128)S(1)} %fusion.38), custom_call_target="Cholesky" | custom-call | tf_op jit(solution)/shard_map/jit(cholesky)/cholesky | solution.py:105
  212.3 19.7 %custom-call.9 = f32[2,1,128,128]{2,3,1,0:T(8,128)S(1)} custom-call(f32[2,1,128,128]{3,2,1,0:T(8,128)S(1)} %select_bitcast_fusion), custom_call_target="InvertDiagBlocksLowerTriangular" | custom-call | tf_op jit(solution)/shard_map/jit(_solve_triangular)/vmap()/triangular_solve | solution.py:107
  232.4 1.2 fusion.41
  233.7 32.2 %convolution_bitcast_fusion = f32[192,128,128]{2,1,0:T(8,128)} fusion(f32[192,384,128]{2,1,0:T(8,128)} %param.6, f32[384,128]{0,1:T(8,128)S(1)} %fusion.41), kind=kOutput, calls=%fused_computation.38 | convolution fusion | flops 14495514624 | bytes 50528256 | tf_op jit(solution)/shard_map/ijk,js->isk/dot_general | solution.py:110
  266.3 21.9 %fusion.15 = f32[128,128,128]{2,0,1:T(8,128)} fusion(f32[192,128,128]{2,1,0:T(8,128)} %convolution_bitcast_fusion, f32[192,128]{1,0:T(8,128)S(1)} %fusion.42), kind=kOutput, calls=%fused_computation.23 | convolution fusion | flops 4831838208 | bytes 21069824 | tf_op jit(solution)/shard_map/ir,isk->rsk/dot_general | solution.py:111
  288.2 71.8 %reduce-scatter.3.cloned.1.call-done = f32[128,32,128]{2,0,1:T(8,128)} async-done(((f32[128,128,128]{2,0,1:T(8,128)}), f32[128,32,128]{2,0,1:T(8,128)}) %reduce-scatter.3.cloned.1.call-update) | async-done | bytes 2097168 | tf_op jit(solution)/shard_map/reduce_scatter | solution.py:112
  360.1 71.8 %reduce-scatter.5.cloned.1.call-done = f32[16,32,128]{2,0,1:T(8,128)} async-done(((f32[128,32,128]{2,0,1:T(8,128)}), f32[16,32,128]{2,0,1:T(8,128)}) %reduce-scatter.5.cloned.1.call-update) | async-done | bytes 262160 | tf_op jit(solution)/shard_map/reduce_scatter | solution.py:113
  431.9 51.9 %all-gather.3.cloned.1.call-done = f32[128,32,128]{2,0,1:T(8,128)} async-done(((f32[16,32,128]{2,0,1:T(8,128)}), f32[128,32,128]{2,0,1:T(8,128)}) %all-gather.3.cloned.1.call-update) | async-done | bytes 2097168 | tf_op jit(solution)/shard_map/all_gather | solution.py:114
  485.2 56.7 %all-gather.5.cloned.1.call-done = f32[128,128,128]{2,0,1:T(8,128)} async-done(((f32[128,32,128]{2,0,1:T(8,128)}), f32[128,128,128]{2,0,1:T(8,128)}) %all-gather.5.cloned.1.call-update) | async-done | bytes 8388624 | tf_op jit(solution)/shard_map/all_gather | solution.py:115
  541.9 4.7 abs_reduce_fusion
  547.3 25.8 %fusion = f32[2,128,128,192]{2,3,1,0:T(8,128)S(1)} fusion(f32[2]{0:T(128)S(1)} %add_divide_fusion, f32[128,128,128]{2,0,1:T(8,128)} %all-gather.5.cloned.1.call-done, f32[192,128]{1,0:T(8,128)S(1)} %fusion.42), kind=kOutput, calls=%fused_computation.6 | convolution fusion | flops 4932501504 | bytes 33652744 | tf_op jit(solution)/shard_map/ir,brsk->bisk/dot_general | solution.py:121
  573.0 29.1 %copy.66 = f32[2,128,128,192]{2,1,3,0:T(8,128)} copy(f32[2,128,128,192]{2,3,1,0:T(8,128)S(1)} %fusion) | data formatting | bytes 50331648 | tf_op jit(solution)/shard_map/ir,brsk->bisk/dot_general | solution.py:121
  602.1 109.8 %shard_map.109 = f32[2,192,10,128]{3,2,1,0:T(8,128)S(1)} custom-call(f32[9]{0:T(128)S(1)} %convert_add_fusion.low_ref, bf16[384,256]{1,0:T(8,128)(2,1)S(1)} %pad_maximum_fusion.1.basis_ref, f32[2,192,128,128]{3,2,1,0:T(8,128)} %bitcast.57), custom_call_target="tpu_custom_call" | custom-call | tf_op jit(solution)/shard_map/pallas_call | solution.py:75
  713.8 1.3 add_multiply_fusion
  715.1 31.5 %all-reduce.10.cloned.1.call-done = f32[2,192,137]{2,1,0:T(8,128)} async-done(((f32[2,192,137]{2,1,0:T(8,128)}), f32[2,192,137]{2,1,0:T(8,128)}) %all-reduce.10.cloned.1.call-update) | async-done | bytes 210448 | tf_op jit(solution)/shard_map/psum | solution.py:129
  746.5 1.1 fusion.34
  748.4 1.6 slice_multiply_fusion
  (58 shorter events, 10.6 us)
Async XLA Ops:
  7.2 0.8 copy-start
  7.2 71.9 %all-reduce.6.cloned.1.call-start = ((), (), s32[]{:S(2)}) async-start(), calls=%async_computation.2 | async-start | bytes 262144 | tf_op jit(solution)/shard_map/psum | solution.py:101
  8.0 36.9 %copy-start.6 = (f32[192,128]{1,0:T(8,128)S(1)}, f32[192,128]{1,0:T(8,128)}, u32[]{:S(2)}) copy-start(f32[192,128]{1,0:T(8,128)} %param.7) | copy-start | bytes 294916
  44.9 109.5 %all-reduce.12.cloned.1.call-start = ((), (), s32[]{:S(2)}) async-start(), calls=%async_computation.9 | async-start | bytes 524288 | tf_op jit(solution)/shard_map/psum | solution.py:103
  81.0 106.6 %all-reduce.8.cloned.1.call-start = ((), (), s32[]{:S(2)}) async-start(), calls=%async_computation.3 | async-start | bytes 131072 | tf_op jit(solution)/shard_map/psum | solution.py:104
  156.4 203.6 %reduce-scatter.3.cloned.1.call-start = ((), (), s32[]{:S(2)}) async-start(), calls=%async_computation.4 | async-start | bytes 10485760 | tf_op jit(solution)/shard_map/reduce_scatter | solution.py:112
  233.7 32.2 %copy-start.2 = (f32[192,128]{0,1:T(8,128)S(1)}, f32[192,128]{0,1:T(8,128)}, u32[]{:S(2)}) copy-start(f32[192,128]{0,1:T(8,128)} %all-reduce.6.cloned.1.call-done) | copy-start | bytes 294916
  266.2 281.0 %copy-start.5 = (f32[192,128]{1,0:T(8,128)}, f32[192,128]{1,0:T(8,128)S(1)}, u32[]{:S(2)}) copy-start(f32[192,128]{1,0:T(8,128)S(1)} %fusion.42) | copy-start | bytes 294916
  266.2 217.7 %copy-start.7 = (s32[9]{0:T(128)S(1)}, s32[9]{0:T(128)}, u32[]{:S(2)}) copy-start(s32[9]{0:T(128)} %param.11) | copy-start | bytes 112
  266.3 280.3 %copy-start.8 = (s32[2]{0:T(128)S(1)}, s32[2]{0:T(128)}, u32[]{:S(2)}) copy-start(s32[2]{0:T(128)} %param.10) | copy-start | bytes 28
  288.2 143.7 %reduce-scatter.5.cloned.1.call-start = ((), (), s32[]{:S(2)}) async-start(), calls=%async_computation.5 | async-start | bytes 2359296 | tf_op jit(solution)/shard_map/reduce_scatter | solution.py:113
  360.1 123.8 %all-gather.3.cloned.1.call-start = ((), (), s32[]{:S(2)}) async-start(), calls=%async_computation.6 | async-start | bytes 2359296 | tf_op jit(solution)/shard_map/all_gather | solution.py:114
  431.9 110.0 %all-gather.5.cloned.1.call-start = ((), (), s32[]{:S(2)}) async-start(), calls=%async_computation.7 | async-start | bytes 10485760 | tf_op jit(solution)/shard_map/all_gather | solution.py:115
  483.9 262.6 %all-reduce.10.cloned.1.call-start = ((), (), s32[]{:S(2)}) async-start(), calls=%async_computation.8 | async-start | bytes 786432 | tf_op jit(solution)/shard_map/psum | solution.py:129
  484.1 89.0 %copy-start.4 = (f32[384,128]{1,0:T(8,128)}, f32[384,128]{1,0:T(8,128)S(1)}, u32[]{:S(2)}) copy-start(f32[384,128]{1,0:T(8,128)S(1)} %copy.40) | copy-start | bytes 589828
  485.2 228.6 %copy-start.3 = (f32[16,32,128]{2,1,0:T(8,128)}, f32[16,32,128]{2,1,0:T(8,128)S(1)}, u32[]{:S(2)}) copy-start(f32[16,32,128]{2,1,0:T(8,128)S(1)} %copy.41) | copy-start | bytes 786436
  602.1 147.9 %copy-start.1 = (f32[128,128]{1,0:T(8,128)S(1)}, f32[128,128]{1,0:T(8,128)}, u32[]{:S(2)}) copy-start(f32[128,128]{1,0:T(8,128)} %param.9) | copy-start | bytes 196612
Sparse Core Ops, SparseCore 0:
  45.0 34.0 all-reduce.5
  83.6 70.7 all-reduce.11
  157.2 30.3 all-reduce.7
  288.3 71.6 reduce-scatter.2
  363.4 68.3 reduce-scatter.4
  433.8 50.0 all-gather.2
  485.4 56.4 all-gather.4
  713.9 32.5 all-reduce.9
